TPU v7x, 512 devices: a whole 4x4x16 slice. The times are simulated.
512 devices in a mesh: ctx: 64 (over y, z_hi, x, core), tp: 8 (over z_lo).
Axes of the slice: x: 4, y: 4, z: 16 (z_hi: 2, z_lo: 8; z = z_hi * 8 + z_lo), core: 2. Of those that a mesh axis runs over, the one named last changes fastest.
Arguments:
- queries: bfloat16 [32768, 3584], P('ctx', 'tp'), may hold values from -4.5 to 4.5
- keys: bfloat16 [32768, 3584], P('ctx', 'tp'), may hold values from -4.5 to 4.5
- values: bfloat16 [32768, 3584], P('ctx', 'tp'), may hold values from -6 to 6
- out_weight: bfloat16 [3584, 3584], P('tp'), may hold values from -0.125 to 0.125
- doc_lengths: int32 [32], replicated, may hold values from 1 to 2048, 32768 in all
Outputs:
- projected: bfloat16 [32768, 3584], P('ctx', 'tp')
Inputs may be any that keep to these rules, and one draw needn't show every extreme that they name: `doc_lengths`: the lengths sum to 32768; the longest document has exactly 2048 tokens.
All inputs are finite; a program needn't handle non-finite values.
Results may differ from a plain program's by a relative error of at most 0.017.
Values may be sent and summed in bfloat16 or wider, within the bound.
A program may use at most 64 MiB of HBM per device.

v0:
```python
import math

import jax
import jax.numpy as jnp
from jax import lax
from jax.sharding import PartitionSpec as P

HD = 112


def passed_along(block, axis, distance):
    devices = range(lax.axis_size(axis))
    route = [(i - distance, i) for i in devices if i - distance in devices]
    return lax.ppermute(block, axis, route)


def doc_of(positions, doc_ends):
    return jnp.sum((positions[:, None] >= doc_ends[None, :]).astype(jnp.int32), axis=1)


def body(queries, keys, values, out_weight, doc_lengths):
    row_count, col_width = queries.shape
    head_count = col_width // HD
    all_heads = head_count * lax.axis_size("tp")
    ctx_count = lax.axis_size("ctx")
    first_pos = lax.axis_index("ctx") * row_count
    query_pos = first_pos + jnp.arange(row_count, dtype=jnp.int32)
    doc_ends = jnp.cumsum(doc_lengths)
    query_doc = doc_of(query_pos, doc_ends)
    head_index = lax.axis_index("tp") * head_count + jnp.arange(head_count, dtype=jnp.int32)
    slopes = 2.0 ** (-4.0 * (head_index.astype(jnp.float32) + 1.0 + all_heads) / all_heads)
    query_heads = queries.reshape(row_count, head_count, HD)

    def attend(current, key_block, value_block, begin_at):
        piece_len = key_block.shape[0]
        key_pos = begin_at + jnp.arange(piece_len, dtype=jnp.int32)
        key_heads = key_block.reshape(piece_len, head_count, HD)
        value_heads = value_block.reshape(piece_len, head_count, HD)
        distance = (query_pos[:, None] - key_pos[None, :]).astype(jnp.float32)
        scores = jnp.einsum(
            "qhd,khd->hqk", query_heads, key_heads, preferred_element_type=jnp.float32
        ) / math.sqrt(HD)
        scores = scores - slopes[:, None, None] * distance[None, :, :]
        allowed = (key_pos[None, :] <= query_pos[:, None]) & (key_pos[None, :] >= 0)
        allowed = allowed & (query_doc[:, None] == doc_of(key_pos, doc_ends)[None, :])
        run_max, run_sum, run_acc = current
        new_max = jnp.maximum(run_max, jnp.max(jnp.where(allowed[None], scores, -1e30), axis=2))
        weights = jnp.where(allowed[None], jnp.exp(scores - new_max[:, :, None]), 0.0)
        factor = jnp.exp(run_max - new_max)
        run_sum = run_sum * factor + jnp.sum(weights, axis=2)
        update = jnp.einsum(
            "hqk,khd->qhd",
            weights.astype(jnp.bfloat16),
            value_heads,
            preferred_element_type=jnp.float32,
        )
        run_acc = run_acc * jnp.transpose(factor)[:, :, None] + update
        return (new_max, run_sum, run_acc)

    def absorb(current, key_block, value_block, begin_at):
        piece_len = key_block.shape[0]
        return attend(current, key_block, value_block, begin_at)

    initial = (
        jnp.full((head_count, row_count), -1e30, jnp.float32),
        jnp.zeros((head_count, row_count), jnp.float32),
        jnp.zeros((row_count, head_count, HD), jnp.float32),
    )
    doc_most = 4 * row_count
    hop_count = min(ctx_count - 1, (doc_most + row_count - 2) // row_count)
    state_now = absorb(initial, keys, values, first_pos)
    stacked = jnp.stack([keys, values])

    def one_hop(number, carried):
        state_in, moving = carried
        moving = passed_along(moving, "ctx", 1)
        state_in = absorb(state_in, moving[0], moving[1], first_pos - number * row_count)
        return (state_in, moving)

    state_now, stacked = lax.fori_loop(1, hop_count + 1, one_hop, (state_now, stacked))
    run_max, run_sum, run_acc = state_now
    attended = (
        (run_acc / jnp.transpose(run_sum)[:, :, None])
        .reshape(row_count, col_width)
        .astype(jnp.bfloat16)
    )
    summed = lax.psum_scatter(
        lax.dot_general(
            out_weight, attended, (((0,), (1,)), ((), ())), preferred_element_type=jnp.float32
        ).astype(jnp.bfloat16),
        "tp",
        scatter_dimension=0,
        tiled=True,
    ).astype(jnp.float32)
    return jnp.transpose(summed).astype(jnp.bfloat16)


def solution(mesh):
    placed = (P("ctx", "tp"), P("ctx", "tp"), P("ctx", "tp"), P("tp", None), P())
    return jax.shard_map(
        body, mesh=mesh, in_specs=placed, out_specs=P("ctx", "tp"), check_vma=False
    )
```

profile of v0, /device:TPU:1, one launch (start us, length us, event | category | flops | bytes accessed | tf_op | source)
XLA Modules:
  0.0 368.5 jit_solution(15883748727787072129)
XLA Ops:
  6.6 0.9 copy.19
  7.6 1.1 subtract_convert_fusion.1
  8.9 0.3 compare_and_fusion.1
  9.2 3.0 select_reduce_fusion.1
  12.2 1.2 fusion.20
  13.5 2.4 fusion.27
  15.9 1.0 pad_maximum_fusion
  16.9 96.7 %while.21 = (s32[]{:T(128)}, f32[4,512]{1,0:T(4,128)S(1)}, f32[4,512]{1,0:T(4,128)S(1)}, f32[512,4,112]{0,2,1:T(8,128)}, bf16[2,512,448]{1,2,0:T(8,128)(2,1)}, /...) while((s32[]{:T(128)}, f32[4,512]{1,0:T(4,128)S(1)}, ...), condition=%wide.region_8.9_spmd.clone.clone, body=%wide.region_4.0_spmd.clone.clone.sunk | while | flops 489676288 | bytes 35870140 | solution.py:80
  16.9 4.5 %collective-permute-start = (bf16[2,512,448]{1,2,0:T(8,128)(2,1)}, bf16[2,512,448]{1,2,0:T(8,128)(2,1)}, u32[]{:S(2)}, u32[]{:S(2)}) collective-permute-start(bf16[2,512,448]{1,2,0:T(8,128)(2,1)} %get-tuple-element.369), channel_id=1, source_target_pairs={{0,8},{8,16},{16,24},{24,32},{32,40},{40,48},{48,56},{56,64},{64,7... | collective-permute-start | bytes 2752520 | tf_op jit(solution)/shard_map/while/body/eval_jaxpr/ppermute | solution.py:14
  21.6 0.3 compare_and_fusion.3
  21.9 0.1 subtract_convert_fusion.3
  22.1 10.0 %collective-permute-done = bf16[2,512,448]{1,2,0:T(8,128)(2,1)} collective-permute-done((bf16[2,512,448]{1,2,0:T(8,128)(2,1)}, bf16[2,512,448]{1,2,0:T(8,128)(2,1)}, u32[]{:S(2)}, u32[]{:S(2)}) %collective-permute-start) | collective-permute-done | bytes 917536 | tf_op jit(solution)/shard_map/while/body/eval_jaxpr/ppermute | solution.py:14
  32.1 1.2 fusion.55
  33.3 2.5 select_reduce_fusion.3
  35.8 1.2 fusion.57
  37.1 1.6 fusion.58
  38.7 2.5 copy.41
  41.2 4.4 %collective-permute-start = (bf16[2,512,448]{1,2,0:T(8,128)(2,1)}, bf16[2,512,448]{1,2,0:T(8,128)(2,1)}, u32[]{:S(2)}, u32[]{:S(2)}) collective-permute-start(bf16[2,512,448]{1,2,0:T(8,128)(2,1)} %get-tuple-element.369), channel_id=1, source_target_pairs={{0,8},{8,16},{16,24},{24,32},{32,40},{40,48},{48,56},{56,64},{64,7... | collective-permute-start | bytes 2752520 | tf_op jit(solution)/shard_map/while/body/eval_jaxpr/ppermute | solution.py:14
  45.7 0.3 compare_and_fusion.3
  46.1 0.1 subtract_convert_fusion.3
  46.2 10.0 %collective-permute-done = bf16[2,512,448]{1,2,0:T(8,128)(2,1)} collective-permute-done((bf16[2,512,448]{1,2,0:T(8,128)(2,1)}, bf16[2,512,448]{1,2,0:T(8,128)(2,1)}, u32[]{:S(2)}, u32[]{:S(2)}) %collective-permute-start) | collective-permute-done | bytes 917536 | tf_op jit(solution)/shard_map/while/body/eval_jaxpr/ppermute | solution.py:14
  56.2 1.2 fusion.55
  57.4 2.5 select_reduce_fusion.3
  59.9 1.2 fusion.57
  61.2 1.6 fusion.58
  62.8 2.5 copy.41
  65.3 4.4 %collective-permute-start = (bf16[2,512,448]{1,2,0:T(8,128)(2,1)}, bf16[2,512,448]{1,2,0:T(8,128)(2,1)}, u32[]{:S(2)}, u32[]{:S(2)}) collective-permute-start(bf16[2,512,448]{1,2,0:T(8,128)(2,1)} %get-tuple-element.369), channel_id=1, source_target_pairs={{0,8},{8,16},{16,24},{24,32},{32,40},{40,48},{48,56},{56,64},{64,7... | collective-permute-start | bytes 2752520 | tf_op jit(solution)/shard_map/while/body/eval_jaxpr/ppermute | solution.py:14
  69.9 0.3 compare_and_fusion.3
  70.2 0.1 subtract_convert_fusion.3
  70.3 10.0 %collective-permute-done = bf16[2,512,448]{1,2,0:T(8,128)(2,1)} collective-permute-done((bf16[2,512,448]{1,2,0:T(8,128)(2,1)}, bf16[2,512,448]{1,2,0:T(8,128)(2,1)}, u32[]{:S(2)}, u32[]{:S(2)}) %collective-permute-start) | collective-permute-done | bytes 917536 | tf_op jit(solution)/shard_map/while/body/eval_jaxpr/ppermute | solution.py:14
  80.3 1.2 fusion.55
  81.6 2.5 select_reduce_fusion.3
  84.1 1.2 fusion.57
  85.4 1.6 fusion.58
  87.0 2.5 copy.41
  89.5 4.4 %collective-permute-start = (bf16[2,512,448]{1,2,0:T(8,128)(2,1)}, bf16[2,512,448]{1,2,0:T(8,128)(2,1)}, u32[]{:S(2)}, u32[]{:S(2)}) collective-permute-start(bf16[2,512,448]{1,2,0:T(8,128)(2,1)} %get-tuple-element.369), channel_id=1, source_target_pairs={{0,8},{8,16},{16,24},{24,32},{32,40},{40,48},{48,56},{56,64},{64,7... | collective-permute-start | bytes 2752520 | tf_op jit(solution)/shard_map/while/body/eval_jaxpr/ppermute | solution.py:14
  94.0 0.3 compare_and_fusion.3
  94.3 0.1 subtract_convert_fusion.3
  94.5 10.0 %collective-permute-done = bf16[2,512,448]{1,2,0:T(8,128)(2,1)} collective-permute-done((bf16[2,512,448]{1,2,0:T(8,128)(2,1)}, bf16[2,512,448]{1,2,0:T(8,128)(2,1)}, u32[]{:S(2)}, u32[]{:S(2)}) %collective-permute-start) | collective-permute-done | bytes 917536 | tf_op jit(solution)/shard_map/while/body/eval_jaxpr/ppermute | solution.py:14
  104.5 1.2 fusion.55
  105.7 2.5 select_reduce_fusion.3
  108.2 1.2 fusion.57
  109.5 1.6 fusion.58
  111.1 2.5 copy.41
  113.6 1.3 divide_convert_fusion
  114.9 3.9 %fusion.18 = bf16[3584,512]{0,1:T(8,128)(2,1)} fusion(bf16[512,448]{0,1:T(8,128)(2,1)S(1)} %bitcast.51, bf16[448,3584]{1,0:T(8,128)(2,1)S(1)} %copy-done), kind=kOutput, calls=%fused_computation.24 | convolution fusion | flops 1646002176 | bytes 7340032 | tf_op jit(solution)/shard_map/dot_general | solution.py:88
  118.8 6.0 %copy.24 = bf16[3584,512]{1,0:T(8,128)(2,1)} copy(bf16[3584,512]{0,1:T(8,128)(2,1)} %fusion.18) | data formatting | bytes 7340032
  124.8 236.9 %reduce-scatter.4.cloned.1.call-done = bf16[448,512]{1,0:T(8,128)(2,1)} async-done(((bf16[3584,512]{1,0:T(8,128)(2,1)}), bf16[448,512]{1,0:T(8,128)(2,1)}) %reduce-scatter.4.cloned.1.call-update) | async-done | bytes 458768
  (62 shorter events, 0.9 us)
Async XLA Ops:
  6.5 108.4 %copy-start = (bf16[448,3584]{1,0:T(8,128)(2,1)S(1)}, bf16[448,3584]{1,0:T(8,128)(2,1)}, u32[]{:S(2)}) copy-start(bf16[448,3584]{1,0:T(8,128)(2,1)} %param.10) | copy-start | bytes 9633796
  6.5 355.1 %reduce-scatter.4.cloned.1.call-start = ((), (), s32[]{:S(2)}) async-start(), calls=%async_computation.1 | async-start | bytes 4128768
  8.8 3.4 copy-start.1
  12.2 1.3 copy-start.5
  13.5 2.4 copy-start.4
  16.9 15.1 %collective-permute-start = (bf16[2,512,448]{1,2,0:T(8,128)(2,1)}, bf16[2,512,448]{1,2,0:T(8,128)(2,1)}, u32[]{:S(2)}, u32[]{:S(2)}) collective-permute-start(bf16[2,512,448]{1,2,0:T(8,128)(2,1)} %get-tuple-element.369), channel_id=1, source_target_pairs={{0,8},{8,16},{16,24},{24,32},{32,40},{40,48},{48,56},{56,64},{64,7... | collective-permute-start | bytes 2752520 | tf_op jit(solution)/shard_map/while/body/eval_jaxpr/ppermute | solution.py:14
  35.8 1.3 copy-start.2
  38.7 2.5 copy-start.3
  41.2 15.0 %collective-permute-start = (bf16[2,512,448]{1,2,0:T(8,128)(2,1)}, bf16[2,512,448]{1,2,0:T(8,128)(2,1)}, u32[]{:S(2)}, u32[]{:S(2)}) collective-permute-start(bf16[2,512,448]{1,2,0:T(8,128)(2,1)} %get-tuple-element.369), channel_id=1, source_target_pairs={{0,8},{8,16},{16,24},{24,32},{32,40},{40,48},{48,56},{56,64},{64,7... | collective-permute-start | bytes 2752520 | tf_op jit(solution)/shard_map/while/body/eval_jaxpr/ppermute | solution.py:14
  59.9 1.3 copy-start.2
  62.8 2.5 copy-start.3
  65.3 15.0 %collective-permute-start = (bf16[2,512,448]{1,2,0:T(8,128)(2,1)}, bf16[2,512,448]{1,2,0:T(8,128)(2,1)}, u32[]{:S(2)}, u32[]{:S(2)}) collective-permute-start(bf16[2,512,448]{1,2,0:T(8,128)(2,1)} %get-tuple-element.369), channel_id=1, source_target_pairs={{0,8},{8,16},{16,24},{24,32},{32,40},{40,48},{48,56},{56,64},{64,7... | collective-permute-start | bytes 2752520 | tf_op jit(solution)/shard_map/while/body/eval_jaxpr/ppermute | solution.py:14
  84.1 1.3 copy-start.2
  87.0 2.5 copy-start.3
  89.5 15.0 %collective-permute-start = (bf16[2,512,448]{1,2,0:T(8,128)(2,1)}, bf16[2,512,448]{1,2,0:T(8,128)(2,1)}, u32[]{:S(2)}, u32[]{:S(2)}) collective-permute-start(bf16[2,512,448]{1,2,0:T(8,128)(2,1)} %get-tuple-element.369), channel_id=1, source_target_pairs={{0,8},{8,16},{16,24},{24,32},{32,40},{40,48},{48,56},{56,64},{64,7... | collective-permute-start | bytes 2752520 | tf_op jit(solution)/shard_map/while/body/eval_jaxpr/ppermute | solution.py:14
  108.2 1.3 copy-start.2
  111.1 2.5 copy-start.3
Sparse Core Ops, SparseCore 0:
  124.9 236.7 reduce-scatter.3
where the time goes:
time: 369 us
  waiting for transfers between devices  277 us (75%)
  matrix products  25.6 us (7%)
  local copies, waits for them, and re-layouts  21.8 us (6%)
  starting transfers between devices  17.6 us (5%)
  between operations  13.5 us (4%)
  other arithmetic  12.7 us (3%)
    unnamed x2, waiting for transfers between devices  237 us
    ppermute x4, waiting for transfers between devices, passed_along(): return lax.ppermute(block, axis, route)  40 us
    ppermute x4, starting transfers between devices, passed_along(): return lax.ppermute(block, axis, route)  17.6 us
    dot_general x5, matrix products, attend(): jnp.einsum('qhd,khd->hqk', query_heads, key_heads, preferred_element_type...  12.9 us
    while x24, local copies, waits for them, and re-layouts  10 us
    dot_general x5, matrix products, attend(): jnp.einsum('hqk,khd->qhd', weights.astype(jnp.bfloat16), value_heads, pre...  8.74 us
  transfers between devices with their start and end apart: 5, of which 5 were waited for; matrix products, arithmetic and copies ran while one was open for 1% of the time, Pallas kernels for 0%

commit v1 on v0

v1 whole, which is shorter than its diff:
```python
import functools
import math

import jax
import jax.numpy as jnp
import numpy as np
from jax import lax
from jax.experimental import pallas as pl
from jax.experimental.pallas import tpu as pltpu
from jax.sharding import PartitionSpec as P

HD = 112
EXTRA = 16
MESH = pl.DeviceIdType.MESH
LOG2E = math.log2(math.e)
NEVER = -1e30
N1, N2, N3, N4, PASS = range(5)
OWN_A, OWN_B, PASSED, SECOND, SIB_OWN, SIB_N2, SIB_N4 = range(7)


def slope_table(all_heads):
    heads = np.arange(all_heads, dtype=np.float64)
    whole = (2.0 ** (-4.0 * (heads + 1.0 + all_heads) / all_heads) * LOG2E).astype(np.float32)
    rest, terms = whole.copy(), []
    for _ in range(3):
        term = rest.astype(jnp.bfloat16).astype(np.float32)
        terms.append(term)
        rest = rest - term
    return np.stack([whole, *terms], axis=1).reshape(-1)


def attend_kernel(
    docs_ref, slopes_ref, q_ref, k_ref, v_ref, o_ref, slot, qx, scores, probs, acc, top, total, send, recv
):
    cols, rows = q_ref.shape
    head_count = cols // HD
    ctx, tp = lax.axis_index("ctx"), lax.axis_index("tp")
    last_seg = lax.axis_size("ctx") // 8 - 1
    seg, x, core = lax.div(ctx, 8), lax.rem(lax.div(ctx, 2), 4), lax.rem(ctx, 2)
    has_next, has_prev = seg < last_seg, seg > 0
    first_pos = ctx * rows

    def at(seg_of, x_of, core_of):
        return (seg_of * 8 + x_of * 2 + core_of, tp)

    sibling = at(seg, x, 1 - core)
    passes = ((x == 0) & (core == 1) | (x == 1) & (core == 0)) & has_next
    ends = x == 3
    a_does = jnp.logical_not(ends) | has_next
    a_seg = jnp.where(ends & (core == 0), seg + 1, seg)
    a_dst = at(a_seg, jnp.where(ends, 0, x + 1), core)
    a_slot = jnp.where(ends & (core == 1), PASS, N2)
    b_does = (x < 2) | (x == 2) & has_next
    b_seg = jnp.where((x == 2) & (core == 1), seg + 1, seg)
    b_dst = at(b_seg, jnp.where(x < 2, x + 2, jnp.where(core == 1, 0, 1)), core)
    b_slot = jnp.where((x == 2) & (core == 0), PASS, N4)
    p_dst = at(seg + 1, 0, core)
    p_slot = jnp.where(core == 1, N2, N4)
    second = (x == 0) & has_prev

    barrier = pltpu.get_barrier_semaphore()

    def greet(condition, device):
        @pl.when(condition)
        def _():
            pl.semaphore_signal(barrier, inc=1, device_id=device, device_id_type=MESH)

    pl.semaphore_signal(barrier, inc=1, device_id=sibling, device_id_type=MESH)
    greet((x > 0), at(seg, x - 1, core))
    greet(second & (core == 0), at(seg - 1, 3, 0))
    greet(second & (core == 1), at(seg - 1, 0, 1))
    greet(x > 1, at(seg, x - 2, core))
    greet((x == 1) & has_prev, at(seg, 0, core))
    greet(second & (core == 1), at(seg - 1, 2, 1))
    greet(second & (core == 0), at(seg - 1, 1, 0))
    greet((x == 0) & (core == 1) & has_next, at(seg, 3, 1))
    greet((x == 1) & (core == 0) & has_next, at(seg, 2, 0))
    awaited = 1 + a_does.astype(jnp.int32) + b_does.astype(jnp.int32)
    awaited = awaited + passes.astype(jnp.int32) + second.astype(jnp.int32)
    pl.semaphore_wait(barrier, awaited)

    def part(ref, head):
        return ref.at[pl.ds(pl.multiple_of(head * HD, 16), HD)]

    def copy(what, src, number, head, kv, device):
        return pltpu.make_async_remote_copy(
            src_ref=part(src, head),
            dst_ref=part(slot.at[number, kv], head),
            send_sem=send.at[what, kv, head],
            recv_sem=recv.at[number, kv, head],
            device_id=device,
            device_id_type=MESH,
        )

    def arrived(number, head, kv):
        copy(SIB_OWN, slot.at[number, kv], number, head, kv, sibling).wait_recv()

    def send_own(head, carry):
        for kv, ref in enumerate((k_ref, v_ref)):

            @pl.when(b_does & (x == 2))
            def _():
                copy(OWN_B, ref, b_slot, head, kv, b_dst).start()

            @pl.when(a_does)
            def _():
                copy(OWN_A, ref, a_slot, head, kv, a_dst).start()

            @pl.when(b_does & (x < 2))
            def _():
                copy(OWN_B, ref, b_slot, head, kv, b_dst).start()

            @pl.when(core == 0)
            def _():
                copy(SIB_OWN, ref, N1, head, kv, sibling).start()

        return carry

    lax.fori_loop(0, head_count, send_own, 0)

    for number in range(4):

        @pl.when(ctx < number + 1)
        def _():
            slot[number] = jnp.zeros(slot.shape[1:], slot.dtype)

    query_at = lax.broadcasted_iota(jnp.int32, (1, rows), 1)
    start = jnp.zeros((1, rows), jnp.int32)
    end = 0
    for doc in range(docs_ref.shape[0]):
        end = end + docs_ref[doc]
        start = jnp.where(end <= query_at + first_pos, end, start)
    start = start - first_pos
    key_at = lax.broadcasted_iota(jnp.int32, (rows, rows), 0)

    extra_row = lax.broadcasted_iota(jnp.int32, (EXTRA, rows), 0)
    extra_col = lax.broadcasted_iota(jnp.int32, (EXTRA, rows), 1)

    def key_rows(number):
        low = lax.rem(extra_col, 16)
        high = extra_col - low - (number + 1) * rows
        ones = jnp.where(extra_row < 9, 1, 0)
        picked = jnp.where(extra_row < 3, high, jnp.where(extra_row < 6, low, ones))
        return picked.astype(jnp.float32).astype(jnp.bfloat16)

    def prepare(head, carry):
        base = (tp * head_count + head) * 4
        whole = slopes_ref[base]
        here = part(q_ref, head)[...].astype(jnp.float32) * (LOG2E / math.sqrt(HD))
        high = here.astype(jnp.bfloat16)
        low = (here - high.astype(jnp.float32)).astype(jnp.bfloat16)
        shift = -whole * extra_col.astype(jnp.float32)
        shift_1 = shift.astype(jnp.bfloat16).astype(jnp.float32)
        shift_2 = (shift - shift_1).astype(jnp.bfloat16).astype(jnp.float32)
        shift_3 = shift - shift_1 - shift_2
        which = lax.rem(extra_row, 3)
        slope = jnp.where(
            which == 0, slopes_ref[base + 1], jnp.where(which == 1, slopes_ref[base + 2], slopes_ref[base + 3])
        )
        moved = jnp.where(which == 0, shift_1, jnp.where(which == 1, shift_2, shift_3))
        rows_of = jnp.where(extra_row < 6, slope, jnp.where(extra_row < 9, moved, 0.0))
        qx[head, pl.ds(0, HD)] = high
        qx[head, pl.ds(HD, EXTRA)] = rows_of.astype(jnp.bfloat16)
        qx[head, pl.ds(HD + EXTRA, HD)] = low
        qx[head, pl.ds(2 * HD + EXTRA, EXTRA)] = jnp.zeros((EXTRA, rows), jnp.bfloat16)
        return carry

    lax.fori_loop(0, head_count, prepare, 0)

    def score(keys, number, head):
        keys = jnp.concatenate([keys, key_rows(number)], axis=0)
        keys = jnp.transpose(keys)
        keys = jnp.concatenate([keys, keys], axis=1)
        return jnp.dot(keys, qx[head], preferred_element_type=jnp.float32)

    def own_block(head, carry):
        for kv in range(2):

            @pl.when(passes)
            def _():
                arrived(PASS, head, kv)
                copy(PASSED, slot.at[PASS, kv], p_slot, head, kv, p_dst).start()

        found = score(part(k_ref, head)[...], -1, head)
        allowed = (key_at <= query_at) & (key_at >= start)
        found = jnp.where(allowed, found, NEVER)
        most = jnp.max(found, axis=0, keepdims=True)
        weights = jnp.exp2(found - most)
        total[head] = jnp.sum(weights, axis=0, keepdims=True)
        top[head] = most
        part(acc, head)[...] = jnp.dot(
            part(v_ref, head)[...], weights.astype(jnp.bfloat16), preferred_element_type=jnp.float32
        )
        return carry

    lax.fori_loop(0, head_count, own_block, 0)

    def bring(head, kv):
        @pl.when(ctx >= 2)
        def _():
            arrived(N2, head, kv)
            copy(SIB_N2, slot.at[N2, kv], jnp.where(core == 0, N3, N1), head, kv, sibling).start()

        @pl.when(second)
        def _():
            copy(SECOND, slot.at[N2, kv], N4, head, kv, at(seg, 1, core)).start()

        @pl.when(ctx >= 4)
        def _():
            arrived(N4, head, kv)

        @pl.when((ctx >= 4) & (core == 1))
        def _():
            copy(SIB_N4, slot.at[N4, kv], N3, head, kv, sibling).start()

        @pl.when(ctx >= 1)
        def _():
            arrived(N1, head, kv)

        @pl.when(ctx >= 3)
        def _():
            arrived(N3, head, kv)

    def earlier_blocks(head, carry):
        bring(head, 0)
        most = top[head]
        for number in range(4):
            found = score(part(slot.at[number, 0], head)[...], number, head)
            found = jnp.where(key_at >= start + (number + 1) * rows, found, NEVER)
            scores[number] = found
            most = jnp.maximum(most, jnp.max(found, axis=0, keepdims=True))
        factor = jnp.exp2(top[head] - most)
        added = total[head] * factor
        for number in range(4):
            weights = jnp.exp2(scores[number] - most)
            added = added + jnp.sum(weights, axis=0, keepdims=True)
            probs[number] = weights.astype(jnp.bfloat16)
        bring(head, 1)
        summed = part(acc, head)[...] * factor
        for number in range(4):
            summed = summed + jnp.dot(
                part(slot.at[number, 1], head)[...], probs[number], preferred_element_type=jnp.float32
            )
        part(o_ref, head)[...] = (summed / added).astype(jnp.bfloat16)
        return carry

    lax.fori_loop(0, head_count, earlier_blocks, 0)

    def sent(head, carry):
        for kv, ref in enumerate((k_ref, v_ref)):
            for what, does in (
                (OWN_A, a_does),
                (OWN_B, b_does),
                (PASSED, passes),
                (SECOND, second),
                (SIB_OWN, core == 0),
                (SIB_N2, ctx >= 2),
                (SIB_N4, (ctx >= 4) & (core == 1)),
            ):

                @pl.when(does)
                def _():
                    copy(what, ref, N1, head, kv, sibling).wait_send()

        return carry

    lax.fori_loop(0, head_count, sent, 0)


def attend(doc_lengths, slopes, queries, keys, values):
    cols, rows = queries.shape
    heads = cols // HD
    bf16, f32 = jnp.bfloat16, jnp.float32
    vmem, smem = pl.BlockSpec(memory_space=pltpu.VMEM), pl.BlockSpec(memory_space=pltpu.SMEM)
    return pl.pallas_call(
        attend_kernel,
        out_shape=jax.ShapeDtypeStruct((cols, rows), bf16),
        in_specs=[smem, smem, vmem, vmem, vmem],
        out_specs=vmem,
        scratch_shapes=[
            pltpu.VMEM((5, 2, cols, rows), bf16),
            pltpu.VMEM((heads, 2 * (HD + EXTRA), rows), bf16),
            pltpu.VMEM((4, rows, rows), f32),
            pltpu.VMEM((4, rows, rows), bf16),
            pltpu.VMEM((cols, rows), f32),
            pltpu.VMEM((heads, 1, rows), f32),
            pltpu.VMEM((heads, 1, rows), f32),
            pltpu.SemaphoreType.DMA((7, 2, heads)),
            pltpu.SemaphoreType.DMA((5, 2, heads)),
        ],
        compiler_params=pltpu.CompilerParams(
            collective_id=0, has_side_effects=True, vmem_limit_bytes=48 << 20
        ),
    )(doc_lengths, slopes, queries, keys, values)


def project_kernel(w_ref, a_ref, o_ref, part, came, send, recv):
    cols, rows = a_ref.shape
    half = rows // 2
    n = part.shape[0]
    ctx, me = lax.axis_index("ctx"), lax.axis_index("tp")
    up, down = (ctx, me + 1), (ctx, me - 1)

    barrier = pltpu.get_barrier_semaphore()

    @pl.when(me > 0)
    def _():
        pl.semaphore_signal(barrier, inc=1, device_id=down, device_id_type=MESH)

    @pl.when(me < n - 1)
    def _():
        pl.semaphore_signal(barrier, inc=1, device_id=up, device_id_type=MESH)

    pl.semaphore_wait(barrier, (me > 0).astype(jnp.int32) + (me < n - 1).astype(jnp.int32))

    def copy(way, owner, piece):
        return pltpu.make_async_remote_copy(
            src_ref=part.at[owner, piece],
            dst_ref=came.at[way, owner, piece],
            send_sem=send.at[owner, piece],
            recv_sem=recv.at[way, owner, piece],
            device_id=up if way == 0 else down,
            device_id_type=MESH,
        )

    def multiply(step, carry):
        pair = jnp.where(me < n // 2, n // 2 - 1 - step, step)
        columns = pl.ds(pl.multiple_of(pair * 2 * cols, 128), 2 * cols)
        found = lax.dot_general(
            w_ref[:, columns], a_ref[...], (((0,), (0,)), ((), ())), preferred_element_type=jnp.float32
        ).astype(jnp.bfloat16)
        for number in range(2):
            for piece in range(2):
                part[2 * pair + number, piece] = found[
                    number * cols : (number + 1) * cols, piece * half : (piece + 1) * half
                ]
        for number in range(2):
            for piece in range(2):

                @pl.when((me == 0) & (2 * pair + 1 - number > 0))
                def _():
                    copy(0, 2 * pair + 1 - number, piece).start()

                @pl.when((me == n - 1) & (2 * pair + number < n - 1))
                def _():
                    copy(1, 2 * pair + number, piece).start()

        return carry

    lax.fori_loop(0, n // 2, multiply, 0)

    def pass_on(way, owner, piece):
        copy(way, owner, piece).wait_recv()
        summed = part[owner, piece].astype(jnp.float32) + came[way, owner, piece].astype(jnp.float32)
        part[owner, piece] = summed.astype(jnp.bfloat16)
        copy(way, owner, piece).start()

    inner = (me > 0) & (me < n - 1)

    def relay(step, carry):
        unit = step - me
        owner = n - 1 - lax.div(unit, 2)

        @pl.when(inner & (unit >= 0) & (owner > me))
        def _():
            pass_on(0, owner, lax.rem(unit, 2))

        unit_down = step - (n - 1 - me)
        owner_down = lax.div(unit_down, 2)

        @pl.when(inner & (unit_down >= 0) & (owner_down < me))
        def _():
            pass_on(1, owner_down, lax.rem(unit_down, 2))

        return carry

    lax.fori_loop(0, 2 * n - 3, relay, 0)

    for piece in range(2):

        @pl.when(me > 0)
        def _():
            copy(0, me, piece).wait_recv()

        @pl.when(me < n - 1)
        def _():
            copy(1, me, piece).wait_recv()

        own = part[me, piece].astype(jnp.float32)
        below = jnp.where(me > 0, came[0, me, piece].astype(jnp.float32), 0.0)
        above = jnp.where(me < n - 1, came[1, me, piece].astype(jnp.float32), 0.0)
        o_ref[:, piece * half : (piece + 1) * half] = (own + below + above).astype(jnp.bfloat16)

    def sent(owner, carry):
        for piece in range(2):

            @pl.when(owner != me)
            def _():
                copy(0, owner, piece).wait_send()

        return carry

    lax.fori_loop(0, n, sent, 0)


def project(out_weight, attended):
    cols, rows = attended.shape
    n = out_weight.shape[1] // cols
    bf16 = jnp.bfloat16
    vmem = pl.BlockSpec(memory_space=pltpu.VMEM)
    return pl.pallas_call(
        project_kernel,
        out_shape=jax.ShapeDtypeStruct((cols, rows), bf16),
        in_specs=[vmem, vmem],
        out_specs=vmem,
        scratch_shapes=[
            pltpu.VMEM((n, 2, cols, rows // 2), bf16),
            pltpu.VMEM((2, n, 2, cols, rows // 2), bf16),
            pltpu.SemaphoreType.DMA((n, 2)),
            pltpu.SemaphoreType.DMA((2, n, 2)),
        ],
        compiler_params=pltpu.CompilerParams(
            collective_id=1, has_side_effects=True, vmem_limit_bytes=48 << 20
        ),
    )(out_weight, attended)


def body(queries, keys, values, out_weight, doc_lengths):
    all_heads = queries.shape[1] // HD * lax.axis_size("tp")
    slopes = jnp.asarray(slope_table(all_heads))
    attended = attend(doc_lengths, slopes, queries.T, keys.T, values.T)
    return project(out_weight, attended).T


def solution(mesh):
    placed = (P("ctx", "tp"), P("ctx", "tp"), P("ctx", "tp"), P("tp", None), P())
    return jax.shard_map(
        body, mesh=mesh, in_specs=placed, out_specs=P("ctx", "tp"), check_vma=False
    )
```

time: 369 us -> 173 us (0.47)
  the two profiles are of different devices: /device:TPU:1 before, /device:TPU:442 now
where the time goes in v1:
time: 173 us
  Pallas kernels  166 us (96%)
  local copies, waits for them, and re-layouts  7.04 us (4%)
    pallas_call x1, Pallas kernels, project(): pl.pallas_call(project_kernel, out_shape=jax.ShapeDtypeStruct((cols, rows...  99.3 us
    pallas_call x1, Pallas kernels, attend(): pl.pallas_call(attend_kernel, out_shape=jax.ShapeDtypeStruct((cols, rows)...  66.6 us
    unnamed x13, local copies, waits for them, and re-layouts  7.04 us

profile of v1, /device:TPU:442, one launch (start us, length us, event | category | flops | bytes accessed | tf_op | source)
XLA Modules:
  0.0 172.9 jit_solution(14522341701954134967)
XLA Ops:
  0.0 0.0 copy-start.1
  0.0 1.0 copy-done.1
  1.0 0.0 copy-start.2
  1.0 1.0 copy-done.2
  2.0 0.0 copy-start.3
  2.0 1.0 copy-done.3
  3.1 0.0 copy-start.4
  3.1 0.7 copy-done.4
  3.7 0.0 copy-start.5
  3.7 0.7 copy-done.5
  4.4 66.6 %shard_map.64.a_ref = bf16[448,512]{1,0:T(8,128)(2,1)S(1)} custom-call(s32[32]{0:T(128)S(1)} %copy-done.4, f32[128]{0:T(128)S(1)} %copy-done.5, bf16[448,512]{1,0:T(8,128)(2,1)S(1)} %bitcast.5, bf16[448,512]{1,0:T(8,128)(2,1)S(1)} %bitcast.6, bf16[448,512]{1,0:T(8,128)(2,1)S(1)} %bitcast.7), custom_call_target="tpu_custom_call" | custom-call | tf_op jit(solution)/shard_map/pallas_call | solution.py:275
  70.9 0.0 copy-start
  71.0 1.9 %copy-done = bf16[448,3584]{1,0:T(8,128)(2,1)S(1)} copy-done((bf16[448,3584]{1,0:T(8,128)(2,1)S(1)}, bf16[448,3584]{1,0:T(8,128)(2,1)}, u32[]{:S(2)}) %copy-start) | copy-done | bytes 3211288
  72.9 99.3 %shard_map.65 = bf16[448,512]{1,0:T(8,128)(2,1)S(1)} custom-call(bf16[448,3584]{1,0:T(8,128)(2,1)S(1)} %copy-done, bf16[448,512]{1,0:T(8,128)(2,1)S(1)} %shard_map.64.a_ref), custom_call_target="tpu_custom_call" | custom-call | tf_op jit(solution)/shard_map/pallas_call | solution.py:411
  172.1 0.8 copy.8
Async XLA Ops:
  0.0 1.0 copy-start.1
  1.0 1.0 copy-start.2
  2.0 1.0 copy-start.3
  3.1 0.7 copy-start.4
  3.7 0.7 copy-start.5
  70.9 1.9 %copy-start = (bf16[448,3584]{1,0:T(8,128)(2,1)S(1)}, bf16[448,3584]{1,0:T(8,128)(2,1)}, u32[]{:S(2)}) copy-start(bf16[448,3584]{1,0:T(8,128)(2,1)} %w_ref.1) | copy-start | bytes 9633796

commit v2 on v1

v2 whole, which is shorter than its diff:
```python
import functools
import math

import jax
import jax.numpy as jnp
import numpy as np
from jax import lax
from jax.experimental import pallas as pl
from jax.experimental.pallas import tpu as pltpu
from jax.sharding import PartitionSpec as P

HD = 112
EXTRA = 16
MESH = pl.DeviceIdType.MESH
LOG2E = math.log2(math.e)
NEVER = -1e30
N1, N2, N3, N4, PASS = range(5)
OWN_A, OWN_B, PASSED, SECOND, SIB_OWN, SIB_N2, SIB_N4 = range(7)
UP, DOWN = range(2)
PIECES = 4


def slope_table(all_heads):
    heads = np.arange(all_heads, dtype=np.float64)
    whole = (2.0 ** (-4.0 * (heads + 1.0 + all_heads) / all_heads) * LOG2E).astype(np.float32)
    rest, terms = whole.copy(), []
    for _ in range(3):
        term = rest.astype(jnp.bfloat16).astype(np.float32)
        terms.append(term)
        rest = rest - term
    return np.stack([whole, *terms], axis=1).reshape(-1)


def weight_rows(cols, y_count):
    return 16 * -(-cols // (16 * 8 * y_count))


def layer_kernel(
    docs_ref, slopes_ref, q_hbm, k_hbm, v_hbm, w_hbm, o_ref,
    q_ref, own, w_ref, slot, qx, scores, probs, acc, top, total,
    wt, wc, first_half, spread, part, came, second_half,
    load, send, recv, z_send, z_recv, x_send, y_send, c_send, w_recv, spread_send, spread_recv, part_send, part_recv, go,
):
    cols, rows = q_ref.shape
    head_count = cols // HD
    n = wt.shape[0]
    piece_len = rows // PIECES
    ctx, me = lax.axis_index("ctx"), lax.axis_index("tp")
    segs = lax.axis_size("ctx") // 8
    y_count = max(1, segs // 2)
    w_rows = weight_rows(cols, y_count)
    seg, x, core = lax.div(ctx, 8), lax.rem(lax.div(ctx, 2), 4), lax.rem(ctx, 2)
    y = lax.div(ctx, 16)
    has_next, has_prev = seg < segs - 1, seg > 0
    first_pos = ctx * rows

    def at(seg_of, x_of, core_of):
        return (seg_of * 8 + x_of * 2 + core_of, me)

    sibling = at(seg, x, 1 - core)
    crosses_a = (x == 3) & (core == 0) & has_next
    crosses_b = (x == 2) & (core == 1) & has_next
    passes = ((x == 0) & (core == 1) | (x == 1) & (core == 0)) & has_next
    ends = x == 3
    a_does = jnp.logical_not(ends) | has_next
    a_seg = jnp.where(ends & (core == 0), seg + 1, seg)
    a_dst = at(a_seg, jnp.where(ends, 0, x + 1), core)
    a_slot = jnp.where(ends & (core == 1), PASS, N2)
    b_does = (x < 2) | (x == 2) & has_next
    b_seg = jnp.where((x == 2) & (core == 1), seg + 1, seg)
    b_dst = at(b_seg, jnp.where(x < 2, x + 2, jnp.where(core == 1, 0, 1)), core)
    b_slot = jnp.where((x == 2) & (core == 0), PASS, N4)
    p_dst = at(seg + 1, 0, core)
    p_slot = jnp.where(core == 1, N2, N4)
    second = (x == 0) & has_prev
    gives = (x == 0) & has_prev
    gives_first = (x == 0) & (seg == 1)
    held = (x >= 2) & has_prev
    if segs > 1:
        held = held | (seg == 0)

    barrier = pltpu.get_barrier_semaphore()

    def greet(condition, device):
        @pl.when(condition)
        def _():
            pl.semaphore_signal(barrier, inc=1, device_id=device, device_id_type=MESH)

    pl.semaphore_signal(barrier, inc=1, device_id=sibling, device_id_type=MESH)
    greet(second & (core == 0), at(seg - 1, 3, 0))
    greet(second & (core == 0), at(seg - 1, 1, 0))
    greet(second & (core == 1), at(seg - 1, 2, 1))
    greet(second & (core == 1), at(seg - 1, 0, 1))
    if segs > 1:
        greet(seg == 0, at(1, 0, core))

    def greet_x(step, carry):
        pl.semaphore_signal(barrier, inc=1, device_id=at(seg, lax.rem(x + step, 4), core), device_id_type=MESH)
        return carry

    lax.fori_loop(1, 4, greet_x, 0)

    def y_at(step):
        return (lax.rem(ctx + step * 16, y_count * 16), me)

    def greet_y(step, carry):
        pl.semaphore_signal(barrier, inc=1, device_id=y_at(step), device_id_type=MESH)
        return carry

    if y_count > 1:
        lax.fori_loop(1, y_count, greet_y, 0)

    def greet_z(step, carry):
        pl.semaphore_signal(barrier, inc=1, device_id=(ctx, lax.rem(me + step, n)), device_id_type=MESH)
        return carry

    lax.fori_loop(1, n, greet_z, 0)

    loads = [
        pltpu.make_async_copy(k_hbm, own.at[0], load.at[0]),
        pltpu.make_async_copy(v_hbm, own.at[1], load.at[1]),
        pltpu.make_async_copy(q_hbm, q_ref, load.at[2]),
        pltpu.make_async_copy(w_hbm, w_ref, load.at[3]),
    ]
    for one in loads:
        one.start()

    crossing = crosses_a.astype(jnp.int32) + crosses_b.astype(jnp.int32) + passes.astype(jnp.int32)
    awaited = 1 + 3 + (y_count - 1) + (n - 1) + crossing + 4 * gives_first.astype(jnp.int32)
    pl.semaphore_wait(barrier, awaited)

    def remote(src, dst, send_sem, recv_sem, device):
        return pltpu.make_async_remote_copy(
            src_ref=src, dst_ref=dst, send_sem=send_sem, recv_sem=recv_sem, device_id=device, device_id_type=MESH
        )

    def part_of(ref, head):
        return ref.at[pl.ds(pl.multiple_of(head * HD, 16), HD)]

    def copy(what, src, number, head, kv, device):
        return remote(
            part_of(src, head),
            part_of(slot.at[number, kv], head),
            send.at[what, kv, head],
            recv.at[number, kv, head],
            device,
        )

    def arrived(number, head, kv):
        copy(SIB_OWN, slot.at[number, kv], number, head, kv, sibling).wait_recv()

    def send_own(head, carry):
        for kv, ref in enumerate((k_hbm, v_hbm)):

            @pl.when(b_does & (x == 2))
            def _():
                copy(OWN_B, ref, b_slot, head, kv, b_dst).start()

            @pl.when(a_does)
            def _():
                copy(OWN_A, ref, a_slot, head, kv, a_dst).start()

            @pl.when(b_does & (x < 2))
            def _():
                copy(OWN_B, ref, b_slot, head, kv, b_dst).start()

            @pl.when(core == 0)
            def _():
                copy(SIB_OWN, ref, N1, head, kv, sibling).start()

        return carry

    def pass_on(head):
        for kv in range(2):

            @pl.when(passes)
            def _():
                arrived(PASS, head, kv)
                copy(PASSED, slot.at[PASS, kv], p_slot, head, kv, p_dst).start()

        @pl.when(passes)
        def _():
            send_own(head, 0)

    @pl.when(jnp.logical_not(passes))
    def _():
        lax.fori_loop(0, head_count, send_own, 0)

    for number in range(4):

        @pl.when(ctx < number + 1)
        def _():
            slot[number] = jnp.zeros(slot.shape[1:], slot.dtype)

    for one in loads:
        one.wait()

    pass_on(0)

    def transpose_pair(pair, carry):
        columns = pl.ds(pl.multiple_of(pair * 2 * cols, 128), 2 * cols)
        found = jnp.transpose(w_ref[:, columns])
        wt[2 * pair] = found[:cols]
        wt[2 * pair + 1] = found[cols:]
        return carry

    lax.fori_loop(0, n // 2, transpose_pair, 0)

    def region(y_of, x_of, core_of):
        return y_of * 8 + core_of * 4 + x_of

    def region_rows(number):
        return pl.ds(pl.multiple_of(number * w_rows, 16), w_rows)

    def there(number):
        return number * w_rows < cols

    mine = region(y, x, core)

    def z_copy(other):
        return remote(
            wt.at[other, region_rows(mine)],
            wc.at[me, region_rows(mine)],
            z_send.at[other],
            z_recv.at[me],
            (ctx, other),
        )

    def z_arrival(other):
        return remote(
            wt.at[other, region_rows(mine)],
            wc.at[other, region_rows(mine)],
            z_send.at[other],
            z_recv.at[other],
            (ctx, other),
        )

    @pl.when(there(mine))
    def _():
        wc[me, region_rows(mine)] = wt[me, region_rows(mine)]

        def start(step, carry):
            z_copy(lax.rem(me + step, n)).start()
            return carry

        lax.fori_loop(1, n, start, 0)

    def w_copy(number, send_sem, device):
        rows_of = region_rows(number)
        return remote(wc.at[:, rows_of], wc.at[:, rows_of], send_sem, w_recv.at[number], device)

    def x_stage():
        @pl.when(there(mine))
        def _():
            def wait(step, carry):
                z_arrival(lax.rem(me + step, n)).wait_recv()
                return carry

            lax.fori_loop(1, n, wait, 0)

            def start(step, carry):
                w_copy(mine, x_send.at[step], at(seg, lax.rem(x + step, 4), core)).start()
                return carry

            lax.fori_loop(1, 4, start, 0)

    def y_stage():
        def one(x_of, carry):
            number = region(y, x_of, core)

            @pl.when(there(number) & (x_of != x))
            def _():
                w_copy(number, x_send.at[0], sibling).wait_recv()

            if y_count > 1:

                @pl.when(there(number))
                def _():
                    def start(step, carry):
                        w_copy(number, y_send.at[x_of, step], y_at(step)).start()
                        return carry

                    lax.fori_loop(1, y_count, start, 0)

            return carry

        lax.fori_loop(0, 4, one, 0)

    def each_lane_region(core_of, do):
        def one(index, carry):
            y_of, x_of = lax.div(index, 4), lax.rem(index, 4)
            number = region(y_of, x_of, core_of)

            @pl.when(there(number))
            def _():
                do(number, y_of)

            return carry

        lax.fori_loop(0, 4 * y_count, one, 0)

    def c_stage():
        def hand_over(number, y_of):
            @pl.when(y_of != y)
            def _():
                w_copy(number, x_send.at[0], sibling).wait_recv()

            w_copy(number, c_send.at[number], sibling).start()

        each_lane_region(core, hand_over)

    def c_arrivals():
        def wait(number, y_of):
            w_copy(number, c_send.at[number], sibling).wait_recv()

        each_lane_region(1 - core, wait)

    def w_sent():
        @pl.when(there(mine))
        def _():
            def z_wait(step, carry):
                z_copy(lax.rem(me + step, n)).wait_send()
                return carry

            lax.fori_loop(1, n, z_wait, 0)

            def x_wait(step, carry):
                w_copy(mine, x_send.at[step], sibling).wait_send()
                return carry

            lax.fori_loop(1, 4, x_wait, 0)

        def y_wait(x_of, carry):
            number = region(y, x_of, core)

            @pl.when(there(number))
            def _():
                def wait(step, carry):
                    w_copy(number, y_send.at[x_of, step], sibling).wait_send()
                    return carry

                lax.fori_loop(1, y_count, wait, 0)

            return carry

        if y_count > 1:
            lax.fori_loop(0, 4, y_wait, 0)
        each_lane_region(core, lambda number, y_of: w_copy(number, c_send.at[number], sibling).wait_send())

    query_at = lax.broadcasted_iota(jnp.int32, (1, rows), 1)
    start = jnp.zeros((1, rows), jnp.int32)
    end = 0
    for doc in range(docs_ref.shape[0]):
        end = end + docs_ref[doc]
        start = jnp.where(end <= query_at + first_pos, end, start)
    start = start - first_pos
    key_at = lax.broadcasted_iota(jnp.int32, (rows, rows), 0)

    extra_row = lax.broadcasted_iota(jnp.int32, (EXTRA, rows), 0)
    extra_col = lax.broadcasted_iota(jnp.int32, (EXTRA, rows), 1)

    def key_rows(number):
        low = lax.rem(extra_col, 16)
        high = extra_col - low - (number + 1) * rows
        ones = jnp.where(extra_row < 9, 1, 0)
        picked = jnp.where(extra_row < 3, high, jnp.where(extra_row < 6, low, ones))
        return picked.astype(jnp.float32).astype(jnp.bfloat16)

    def prepare(head, carry):
        base = (me * head_count + head) * 4
        whole = slopes_ref[base]
        here = part_of(q_ref, head)[...].astype(jnp.float32) * (LOG2E / math.sqrt(HD))
        high = here.astype(jnp.bfloat16)
        low = (here - high.astype(jnp.float32)).astype(jnp.bfloat16)
        shift = -whole * extra_col.astype(jnp.float32)
        shift_1 = shift.astype(jnp.bfloat16).astype(jnp.float32)
        shift_2 = (shift - shift_1).astype(jnp.bfloat16).astype(jnp.float32)
        shift_3 = shift - shift_1 - shift_2
        which = lax.rem(extra_row, 3)
        slope = jnp.where(
            which == 0, slopes_ref[base + 1], jnp.where(which == 1, slopes_ref[base + 2], slopes_ref[base + 3])
        )
        moved = jnp.where(which == 0, shift_1, jnp.where(which == 1, shift_2, shift_3))
        rows_of = jnp.where(extra_row < 6, slope, jnp.where(extra_row < 9, moved, 0.0))
        qx[head, pl.ds(0, HD)] = high
        qx[head, pl.ds(HD, EXTRA)] = rows_of.astype(jnp.bfloat16)
        qx[head, pl.ds(HD + EXTRA, HD)] = low
        qx[head, pl.ds(2 * HD + EXTRA, EXTRA)] = jnp.zeros((EXTRA, rows), jnp.bfloat16)
        return carry

    lax.fori_loop(0, head_count, prepare, 0)

    def score(keys, number, head):
        keys = jnp.concatenate([keys, key_rows(number)], axis=0)
        keys = jnp.transpose(keys)
        keys = jnp.concatenate([keys, keys], axis=1)
        return jnp.dot(keys, qx[head], preferred_element_type=jnp.float32)

    def own_block(head, carry):
        @pl.when(head > 0)
        def _():
            pass_on(head)

        found = score(part_of(own.at[0], head)[...], -1, head)
        allowed = (key_at <= query_at) & (key_at >= start)
        found = jnp.where(allowed, found, NEVER)
        most = jnp.max(found, axis=0, keepdims=True)
        weights = jnp.exp2(found - most)
        total[head] = jnp.sum(weights, axis=0, keepdims=True)
        top[head] = most
        part_of(acc, head)[...] = jnp.dot(
            part_of(own.at[1], head)[...], weights.astype(jnp.bfloat16), preferred_element_type=jnp.float32
        )
        return carry

    lax.fori_loop(0, head_count, own_block, 0)
    x_stage()

    def bring(head, kv):
        @pl.when(ctx >= 2)
        def _():
            arrived(N2, head, kv)
            copy(SIB_N2, slot.at[N2, kv], jnp.where(core == 0, N3, N1), head, kv, sibling).start()

        @pl.when(second)
        def _():
            copy(SECOND, slot.at[N2, kv], N4, head, kv, at(seg, 1, core)).start()

        @pl.when(ctx >= 4)
        def _():
            arrived(N4, head, kv)

        @pl.when((ctx >= 4) & (core == 1))
        def _():
            copy(SIB_N4, slot.at[N4, kv], N3, head, kv, sibling).start()

        @pl.when(ctx >= 1)
        def _():
            arrived(N1, head, kv)

        @pl.when(ctx >= 3)
        def _():
            arrived(N3, head, kv)

    def earlier_blocks(head, carry):
        bring(head, 0)
        most = top[head]
        for number in range(4):
            found = score(part_of(slot.at[number, 0], head)[...], number, head)
            found = jnp.where(key_at >= start + (number + 1) * rows, found, NEVER)
            scores[number] = found
            most = jnp.maximum(most, jnp.max(found, axis=0, keepdims=True))
        factor = jnp.exp2(top[head] - most)
        added = total[head] * factor
        for number in range(4):
            weights = jnp.exp2(scores[number] - most)
            added = added + jnp.sum(weights, axis=0, keepdims=True)
            probs[number] = weights.astype(jnp.bfloat16)
        bring(head, 1)

        @pl.when((head == head_count - 1) & gives)
        def _():
            for x_of in (2, 3):
                pl.semaphore_signal(go, inc=1, device_id=at(seg, x_of, core), device_id_type=MESH)

        @pl.when((head == head_count - 1) & gives_first)
        def _():
            for x_of in range(4):
                pl.semaphore_signal(go, inc=1, device_id=at(0, x_of, core), device_id_type=MESH)

        summed = part_of(acc, head)[...] * factor
        for number in range(4):
            summed = summed + jnp.dot(
                part_of(slot.at[number, 1], head)[...], probs[number], preferred_element_type=jnp.float32
            )
        attended = (summed / added).astype(jnp.bfloat16)
        part_of(first_half, head)[...] = attended[:, : 2 * piece_len]
        for piece in range(2):
            part_of(spread.at[me, piece], head)[...] = attended[:, (2 + piece) * piece_len : (3 + piece) * piece_len]

        @pl.when(head == 0)
        def _():
            y_stage()

        return carry

    lax.fori_loop(0, head_count, earlier_blocks, 0)

    @pl.when(held)
    def _():
        pl.semaphore_wait(go, 1)

    places = ((ctx, me + 1), (ctx, me - 1))
    below = (me, n - 1 - me)

    def spread_copy(way, source, piece):
        ref = spread.at[source, piece]
        return remote(ref, ref, spread_send.at[way, source, piece], spread_recv.at[source, piece], places[way])

    def part_copy(way, owner, piece):
        return remote(
            part.at[owner, piece],
            came.at[way, owner, piece],
            part_send.at[owner, piece],
            part_recv.at[way, owner, piece],
            places[way],
        )

    for piece in range(2):
        for way in (UP, DOWN):

            @pl.when(below[way] < n - 1)
            def _():
                spread_copy(way, me, piece).start()

    c_stage()

    def partials(owner, carry):
        found = jnp.dot(wt[owner], first_half[...], preferred_element_type=jnp.float32).astype(jnp.bfloat16)
        for piece in range(2):
            part[owner, piece] = found[:, piece * piece_len : (piece + 1) * piece_len]
        return carry

    lax.fori_loop(0, n, partials, 0)
    for piece in range(2):
        second_half[piece] = jnp.dot(wt[me], spread[me, piece], preferred_element_type=jnp.float32)
    c_arrivals()

    def slot_of(time, carry):
        number, piece = lax.div(time, 2), lax.rem(time, 2)
        for way in (UP, DOWN):
            behind = below[way]
            sign = 1 - 2 * way
            source = me - sign * number

            @pl.when(number <= behind)
            def _():
                spread_copy(way, source, piece).wait_recv()

            @pl.when((number <= behind) & (behind < n - 1))
            def _():
                spread_copy(way, source, piece).start()

            owner = jnp.where(way == UP, n - 1, 0) - sign * (number - behind - 1)
            sums = (number > behind) & (behind < n - 1)

            @pl.when(sums & (behind > 0))
            def _():
                part_copy(way, owner, piece).wait_recv()
                summed = part[owner, piece].astype(jnp.float32) + came[way, owner, piece].astype(jnp.float32)
                part[owner, piece] = summed.astype(jnp.bfloat16)

            @pl.when(sums)
            def _():
                part_copy(way, owner, piece).start()

        for way in (UP, DOWN):
            source = me - (1 - 2 * way) * number

            @pl.when(number <= below[way])
            def _():
                second_half[piece] += jnp.dot(wc[source], spread[source, piece], preferred_element_type=jnp.float32)

        return carry

    lax.fori_loop(2, 2 * n, slot_of, 0)

    for piece in range(2):
        for way in (UP, DOWN):

            @pl.when(below[way] > 0)
            def _():
                part_copy(way, me, piece).wait_recv()

        whole = part[me, piece].astype(jnp.float32)
        for way in (UP, DOWN):
            whole = whole + jnp.where(below[way] > 0, came[way, me, piece].astype(jnp.float32), 0.0)
        o_ref[:, piece * piece_len : (piece + 1) * piece_len] = whole.astype(jnp.bfloat16)
        o_ref[:, (2 + piece) * piece_len : (3 + piece) * piece_len] = second_half[piece].astype(jnp.bfloat16)

    def sent(head, carry):
        for kv, ref in enumerate((k_hbm, v_hbm)):
            for what, does in (
                (OWN_A, a_does),
                (OWN_B, b_does),
                (PASSED, passes),
                (SECOND, second),
                (SIB_OWN, core == 0),
                (SIB_N2, ctx >= 2),
                (SIB_N4, (ctx >= 4) & (core == 1)),
            ):

                @pl.when(does)
                def _():
                    copy(what, ref, N1, head, kv, sibling).wait_send()

        return carry

    lax.fori_loop(0, head_count, sent, 0)
    w_sent()

    def sums_sent(other, carry):
        for piece in range(2):

            @pl.when(other != me)
            def _():
                part_copy(UP, other, piece).wait_send()

            for way in (UP, DOWN):
                sign = 1 - 2 * way
                passed = (below[way] < n - 1) & ((me - other) * sign >= 0)

                @pl.when(passed)
                def _():
                    spread_copy(way, other, piece).wait_send()

        return carry

    lax.fori_loop(0, n, sums_sent, 0)


def layer(doc_lengths, slopes, queries, keys, values, out_weight):
    cols, rows = queries.shape
    heads = cols // HD
    n = out_weight.shape[1] // cols
    y_count = max(1, lax.axis_size("ctx") // 16)
    regions = 8 * y_count
    piece = rows // PIECES
    bf16, f32 = jnp.bfloat16, jnp.float32
    vmem, smem = pl.BlockSpec(memory_space=pltpu.VMEM), pl.BlockSpec(memory_space=pltpu.SMEM)
    anywhere = pl.BlockSpec(memory_space=pl.ANY)
    dma = pltpu.SemaphoreType.DMA
    return pl.pallas_call(
        layer_kernel,
        out_shape=jax.ShapeDtypeStruct((cols, rows), bf16),
        in_specs=[smem, smem, anywhere, anywhere, anywhere, anywhere],
        out_specs=vmem,
        scratch_shapes=[
            pltpu.VMEM((cols, rows), bf16),
            pltpu.VMEM((2, cols, rows), bf16),
            pltpu.VMEM((cols, n * cols), bf16),
            pltpu.VMEM((5, 2, cols, rows), bf16),
            pltpu.VMEM((heads, 2 * (HD + EXTRA), rows), bf16),
            pltpu.VMEM((4, rows, rows), f32),
            pltpu.VMEM((4, rows, rows), bf16),
            pltpu.VMEM((cols, rows), f32),
            pltpu.VMEM((heads, 1, rows), f32),
            pltpu.VMEM((heads, 1, rows), f32),
            pltpu.VMEM((n, cols, cols), bf16),
            pltpu.VMEM((n, cols, cols), bf16),
            pltpu.VMEM((cols, 2 * piece), bf16),
            pltpu.VMEM((n, 2, cols, piece), bf16),
            pltpu.VMEM((n, 2, cols, piece), bf16),
            pltpu.VMEM((2, n, 2, cols, piece), bf16),
            pltpu.VMEM((2, cols, piece), f32),
            dma((4,)),
            dma((7, 2, heads)),
            dma((5, 2, heads)),
            dma((n,)),
            dma((n,)),
            dma((4,)),
            dma((4, y_count)),
            dma((regions,)),
            dma((regions,)),
            dma((2, n, 2)),
            dma((n, 2)),
            dma((n, 2)),
            dma((2, n, 2)),
            pltpu.SemaphoreType.REGULAR,
        ],
        compiler_params=pltpu.CompilerParams(
            collective_id=0, has_side_effects=True, vmem_limit_bytes=56 << 20
        ),
    )(doc_lengths, slopes, queries, keys, values, out_weight)


def body(queries, keys, values, out_weight, doc_lengths):
    all_heads = queries.shape[1] // HD * lax.axis_size("tp")
    slopes = jnp.asarray(slope_table(all_heads))
    return layer(doc_lengths, slopes, queries.T, keys.T, values.T, out_weight).T


def solution(mesh):
    placed = (P("ctx", "tp"), P("ctx", "tp"), P("ctx", "tp"), P("tp", None), P())
    return jax.shard_map(
        body, mesh=mesh, in_specs=placed, out_specs=P("ctx", "tp"), check_vma=False
    )
```

time: 173 us -> 148 us (0.86)
  the two profiles are of different devices: /device:TPU:442 before, /device:TPU:26 now
where the time goes in v2:
time: 148 us
  Pallas kernels  146 us (99%)
  local copies, waits for them, and re-layouts  1.82 us (1%)
    pallas_call x1, Pallas kernels, layer(): pl.pallas_call(layer_kernel, out_shape=jax.ShapeDtypeStruct((cols, rows),...  146 us

profile of v2, /device:TPU:26, one launch (start us, length us, event | category | flops | bytes accessed | tf_op | source)
XLA Modules:
  0.0 147.6 jit_solution(18088922981150598567)
XLA Ops:
  0.0 145.8 %shard_map.64 = bf16[448,512]{1,0:T(8,128)(2,1)} custom-call(s32[32]{0:T(128)} %docs_ref.1, f32[128]{0:T(128)} %constant.2.clone.slopes_ref, bf16[448,512]{1,0:T(8,128)(2,1)} %bitcast.5, bf16[448,512]{1,0:T(8,128)(2,1)} %bitcast.6, bf16[448,512]{1,0:T(8,128)(2,1)} %bitcast.7, bf16[448,3584]{1,0:T(8,128)(2,1)} %w_hbm.1), custom_call_target="tpu_custom_call" | custom-call | tf_op jit(solution)/shard_map/pallas_call | solution.py:633
  145.8 1.8 %copy.8 = bf16[512,448]{0,1:T(8,128)(2,1)} copy(bf16[512,448]{0,1:T(8,128)(2,1)} %bitcast.4) | data formatting | bytes 917504

commit v3 on v2

--- a/solution.py
+++ b/solution.py
@@ -15,7 +15,7 @@
 LOG2E = math.log2(math.e)
 NEVER = -1e30
 N1, N2, N3, N4, PASS = range(5)
-OWN_A, OWN_B, PASSED, SECOND, SIB_OWN, SIB_N2, SIB_N4 = range(7)
+OWN_A, OWN_B, CROSSES, PASSED, SECOND, SIB_OWN, SIB_N2, SIB_N4 = range(8)
 UP, DOWN = range(2)
 PIECES = 4
 
@@ -58,21 +58,22 @@
         return (seg_of * 8 + x_of * 2 + core_of, me)
 
     sibling = at(seg, x, 1 - core)
-    crosses_a = (x == 3) & (core == 0) & has_next
-    crosses_b = (x == 2) & (core == 1) & has_next
-    passes = ((x == 0) & (core == 1) | (x == 1) & (core == 0)) & has_next
-    ends = x == 3
-    a_does = jnp.logical_not(ends) | has_next
-    a_seg = jnp.where(ends & (core == 0), seg + 1, seg)
-    a_dst = at(a_seg, jnp.where(ends, 0, x + 1), core)
-    a_slot = jnp.where(ends & (core == 1), PASS, N2)
-    b_does = (x < 2) | (x == 2) & has_next
-    b_seg = jnp.where((x == 2) & (core == 1), seg + 1, seg)
-    b_dst = at(b_seg, jnp.where(x < 2, x + 2, jnp.where(core == 1, 0, 1)), core)
-    b_slot = jnp.where((x == 2) & (core == 0), PASS, N4)
-    p_dst = at(seg + 1, 0, core)
-    p_slot = jnp.where(core == 1, N2, N4)
-    second = (x == 0) & has_prev
+    upper = lax.rem(seg, 2) == 1
+    crosses = (x >= 2) & has_next
+    on_column = lax.rem(x, 2) != core
+    goes_round = crosses & on_column & jnp.logical_not(upper)
+    pass_x = jnp.where(x == 3, jnp.where(core == 1, 0, 3), jnp.where(core == 1, 2, 1))
+    x_slot = jnp.where((x == 0) | (x == 3), N2, N4)
+    c_dst = at(
+        jnp.where(goes_round, seg + 1, jnp.where(upper, seg + 2, seg)), jnp.where(goes_round, 0, pass_x), core
+    )
+    c_slot = jnp.where(goes_round, x_slot, PASS)
+    passes = on_column & (jnp.where(upper, seg, 0) != 1) & (upper | (x < 2) & has_next)
+    p_source = at(jnp.where(upper, seg - 2, seg), jnp.where((x == 0) | (x == 3), 3, 2), core)
+    p_dst = at(jnp.where(upper, seg - 1, seg + 1), 0, core)
+    a_does = x < 3
+    b_does = x == 1
+    second = (x == 0) & has_prev | (x == 1)
     gives = (x == 0) & has_prev
     gives_first = (x == 0) & (seg == 1)
     held = (x >= 2) & has_prev
@@ -87,11 +88,10 @@
             pl.semaphore_signal(barrier, inc=1, device_id=device, device_id_type=MESH)
 
     pl.semaphore_signal(barrier, inc=1, device_id=sibling, device_id_type=MESH)
-    greet(second & (core == 0), at(seg - 1, 3, 0))
-    greet(second & (core == 0), at(seg - 1, 1, 0))
-    greet(second & (core == 1), at(seg - 1, 2, 1))
-    greet(second & (core == 1), at(seg - 1, 0, 1))
     if segs > 1:
+        greet(passes, p_source)
+        for x_of in (jnp.where(core == 1, 0, 3), jnp.where(core == 1, 2, 1)):
+            greet((x == 0) & has_prev, at(jnp.where(upper, seg - 1, seg + 1), x_of, core))
         greet(seg == 0, at(1, 0, core))
 
     def greet_x(step, carry):
@@ -125,7 +125,7 @@
     for one in loads:
         one.start()
 
-    crossing = crosses_a.astype(jnp.int32) + crosses_b.astype(jnp.int32) + passes.astype(jnp.int32)
+    crossing = crosses.astype(jnp.int32) + passes.astype(jnp.int32)
     awaited = 1 + 3 + (y_count - 1) + (n - 1) + crossing + 4 * gives_first.astype(jnp.int32)
     pl.semaphore_wait(barrier, awaited)
 
@@ -152,17 +152,13 @@
     def send_own(head, carry):
         for kv, ref in enumerate((k_hbm, v_hbm)):
 
-            @pl.when(b_does & (x == 2))
-            def _():
-                copy(OWN_B, ref, b_slot, head, kv, b_dst).start()
-
             @pl.when(a_does)
             def _():
-                copy(OWN_A, ref, a_slot, head, kv, a_dst).start()
-
-            @pl.when(b_does & (x < 2))
-            def _():
-                copy(OWN_B, ref, b_slot, head, kv, b_dst).start()
+                copy(OWN_A, ref, N2, head, kv, at(seg, x + 1, core)).start()
+
+            @pl.when(b_does)
+            def _():
+                copy(OWN_B, ref, N4, head, kv, at(seg, x + 2, core)).start()
 
             @pl.when(core == 0)
             def _():
@@ -170,22 +166,28 @@
 
         return carry
 
-    def pass_on(head):
+    def send_over(head, carry):
+        for kv, ref in enumerate((k_hbm, v_hbm)):
+
+            @pl.when(crosses)
+            def _():
+                copy(CROSSES, ref, c_slot, head, kv, c_dst).start()
+
+        return carry
+
+    def pass_on(head, carry):
         for kv in range(2):
 
             @pl.when(passes)
             def _():
                 arrived(PASS, head, kv)
-                copy(PASSED, slot.at[PASS, kv], p_slot, head, kv, p_dst).start()
-
-        @pl.when(passes)
-        def _():
-            send_own(head, 0)
-
-    @pl.when(jnp.logical_not(passes))
-    def _():
-        lax.fori_loop(0, head_count, send_own, 0)
-
+                copy(PASSED, slot.at[PASS, kv], x_slot, head, kv, p_dst).start()
+
+        return carry
+
+    lax.fori_loop(0, head_count, send_over, 0)
+    lax.fori_loop(0, head_count, send_own, 0)
+    lax.fori_loop(0, head_count, pass_on, 0)
     for number in range(4):
 
         @pl.when(ctx < number + 1)
@@ -194,8 +196,6 @@
 
     for one in loads:
         one.wait()
-
-    pass_on(0)
 
     def transpose_pair(pair, carry):
         columns = pl.ds(pl.multiple_of(pair * 2 * cols, 128), 2 * cols)
@@ -397,9 +397,12 @@
         return jnp.dot(keys, qx[head], preferred_element_type=jnp.float32)
 
     def own_block(head, carry):
-        @pl.when(head > 0)
-        def _():
-            pass_on(head)
+        for kv in range(2):
+
+            @pl.when(x == 1)
+            def _():
+                arrived(N2, head, kv)
+                copy(SECOND, slot.at[N2, kv], N4, head, kv, at(seg, 2, core)).start()
 
         found = score(part_of(own.at[0], head)[...], -1, head)
         allowed = (key_at <= query_at) & (key_at >= start)
@@ -415,14 +418,18 @@
 
     lax.fori_loop(0, head_count, own_block, 0)
     x_stage()
+    y_stage()
 
     def bring(head, kv):
+        @pl.when((ctx >= 2) & (x != 1))
+        def _():
+            arrived(N2, head, kv)
+
         @pl.when(ctx >= 2)
         def _():
-            arrived(N2, head, kv)
             copy(SIB_N2, slot.at[N2, kv], jnp.where(core == 0, N3, N1), head, kv, sibling).start()
 
-        @pl.when(second)
+        @pl.when((x == 0) & has_prev)
         def _():
             copy(SECOND, slot.at[N2, kv], N4, head, kv, at(seg, 1, core)).start()
 
@@ -478,10 +485,6 @@
         for piece in range(2):
             part_of(spread.at[me, piece], head)[...] = attended[:, (2 + piece) * piece_len : (3 + piece) * piece_len]
 
-        @pl.when(head == 0)
-        def _():
-            y_stage()
-
         return carry
 
     lax.fori_loop(0, head_count, earlier_blocks, 0)
@@ -524,8 +527,6 @@
     lax.fori_loop(0, n, partials, 0)
     for piece in range(2):
         second_half[piece] = jnp.dot(wt[me], spread[me, piece], preferred_element_type=jnp.float32)
-    c_arrivals()
-
     def slot_of(time, carry):
         number, piece = lax.div(time, 2), lax.rem(time, 2)
         for way in (UP, DOWN):
@@ -554,6 +555,12 @@
             def _():
                 part_copy(way, owner, piece).start()
 
+        return carry
+
+    lag = min(4, 2 * n - 2)
+
+    def product(time, carry):
+        number, piece = lax.div(time, 2), lax.rem(time, 2)
         for way in (UP, DOWN):
             source = me - (1 - 2 * way) * number
 
@@ -563,7 +570,10 @@
 
         return carry
 
-    lax.fori_loop(2, 2 * n, slot_of, 0)
+    lax.fori_loop(2, 2 + lag, slot_of, 0)
+    c_arrivals()
+    lax.fori_loop(2 + lag, 2 * n, lambda time, carry: product(time - lag, slot_of(time, carry)), 0)
+    lax.fori_loop(2 * n - lag, 2 * n, product, 0)
 
     for piece in range(2):
         for way in (UP, DOWN):
@@ -583,6 +593,7 @@
             for what, does in (
                 (OWN_A, a_does),
                 (OWN_B, b_does),
+                (CROSSES, crosses),
                 (PASSED, passes),
                 (SECOND, second),
                 (SIB_OWN, core == 0),
@@ -654,7 +665,7 @@
             pltpu.VMEM((2, n, 2, cols, piece), bf16),
             pltpu.VMEM((2, cols, piece), f32),
             dma((4,)),
-            dma((7, 2, heads)),
+            dma((8, 2, heads)),
             dma((5, 2, heads)),
             dma((n,)),
             dma((n,)),

time: 148 us -> 149 us (level)
  the two profiles are of different devices: /device:TPU:26 before, /device:TPU:4 now
where the time goes in v3:
time: 149 us
  Pallas kernels  147 us (99%)
  local copies, waits for them, and re-layouts  1.82 us (1%)
    pallas_call x1, Pallas kernels, layer(): pl.pallas_call(layer_kernel, out_shape=jax.ShapeDtypeStruct((cols, rows),...  147 us

profile of v3, /device:TPU:4, one launch (start us, length us, event | category | flops | bytes accessed | tf_op | source)
XLA Modules:
  0.0 148.5 jit_solution(474225224061615418)
XLA Ops:
  0.0 146.7 %shard_map.64 = bf16[448,512]{1,0:T(8,128)(2,1)} custom-call(s32[32]{0:T(128)} %docs_ref.1, f32[128]{0:T(128)} %constant.2.clone.slopes_ref, bf16[448,512]{1,0:T(8,128)(2,1)} %bitcast.5, bf16[448,512]{1,0:T(8,128)(2,1)} %bitcast.6, bf16[448,512]{1,0:T(8,128)(2,1)} %bitcast.7, bf16[448,3584]{1,0:T(8,128)(2,1)} %w_hbm.1), custom_call_target="tpu_custom_call" | custom-call | tf_op jit(solution)/shard_map/pallas_call | solution.py:644
  146.7 1.8 %copy.8 = bf16[512,448]{0,1:T(8,128)(2,1)} copy(bf16[512,448]{0,1:T(8,128)(2,1)} %bitcast.4) | data formatting | bytes 917504

commit v4 on v3

--- a/solution.py
+++ b/solution.py
@@ -39,7 +39,7 @@
     docs_ref, slopes_ref, q_hbm, k_hbm, v_hbm, w_hbm, o_ref,
     q_ref, own, w_ref, slot, qx, scores, probs, acc, top, total,
     wt, wc, first_half, spread, part, came, second_half,
-    load, send, recv, z_send, z_recv, x_send, y_send, c_send, w_recv, spread_send, spread_recv, part_send, part_recv, go,
+    load, send, recv, z_send, z_recv, x_send, y_send, c_send, w_recv, spread_send, spread_recv, part_send, part_recv,
 ):
     cols, rows = q_ref.shape
     head_count = cols // HD
@@ -74,11 +74,6 @@
     a_does = x < 3
     b_does = x == 1
     second = (x == 0) & has_prev | (x == 1)
-    gives = (x == 0) & has_prev
-    gives_first = (x == 0) & (seg == 1)
-    held = (x >= 2) & has_prev
-    if segs > 1:
-        held = held | (seg == 0)
 
     barrier = pltpu.get_barrier_semaphore()
 
@@ -92,7 +87,6 @@
         greet(passes, p_source)
         for x_of in (jnp.where(core == 1, 0, 3), jnp.where(core == 1, 2, 1)):
             greet((x == 0) & has_prev, at(jnp.where(upper, seg - 1, seg + 1), x_of, core))
-        greet(seg == 0, at(1, 0, core))
 
     def greet_x(step, carry):
         pl.semaphore_signal(barrier, inc=1, device_id=at(seg, lax.rem(x + step, 4), core), device_id_type=MESH)
@@ -125,14 +119,62 @@
     for one in loads:
         one.start()
 
+    loads[3].wait()
+    def transpose_pair(pair, carry):
+        columns = pl.ds(pl.multiple_of(pair * 2 * cols, 128), 2 * cols)
+        found = jnp.transpose(w_ref[:, columns])
+        wt[2 * pair, :, :cols] = found[:cols]
+        wt[2 * pair + 1, :, :cols] = found[cols:]
+        return carry
+
+    lax.fori_loop(0, n // 2, transpose_pair, 0)
     crossing = crosses.astype(jnp.int32) + passes.astype(jnp.int32)
-    awaited = 1 + 3 + (y_count - 1) + (n - 1) + crossing + 4 * gives_first.astype(jnp.int32)
+    awaited = 1 + 3 + (y_count - 1) + (n - 1) + crossing
     pl.semaphore_wait(barrier, awaited)
 
     def remote(src, dst, send_sem, recv_sem, device):
         return pltpu.make_async_remote_copy(
             src_ref=src, dst_ref=dst, send_sem=send_sem, recv_sem=recv_sem, device_id=device, device_id_type=MESH
         )
+
+    def region(y_of, x_of, core_of):
+        return y_of * 8 + core_of * 4 + x_of
+
+    def region_rows(number):
+        return pl.ds(pl.multiple_of(number * w_rows, 16), w_rows)
+
+    def there(number):
+        return number * w_rows < cols
+
+    mine = region(y, x, core)
+
+    def z_copy(other):
+        return remote(
+            wt.at[other, region_rows(mine)],
+            wc.at[me, region_rows(mine)],
+            z_send.at[other],
+            z_recv.at[me],
+            (ctx, other),
+        )
+
+    def z_arrival(other):
+        return remote(
+            wt.at[other, region_rows(mine)],
+            wc.at[other, region_rows(mine)],
+            z_send.at[other],
+            z_recv.at[other],
+            (ctx, other),
+        )
+
+    @pl.when(there(mine))
+    def _():
+        wc[me, region_rows(mine)] = wt[me, region_rows(mine)]
+
+        def start(step, carry):
+            z_copy(lax.rem(me + step, n)).start()
+            return carry
+
+        lax.fori_loop(1, n, start, 0)
 
     def part_of(ref, head):
         return ref.at[pl.ds(pl.multiple_of(head * HD, 16), HD)]
@@ -149,6 +191,15 @@
     def arrived(number, head, kv):
         copy(SIB_OWN, slot.at[number, kv], number, head, kv, sibling).wait_recv()
 
+    def send_sibling(head, carry):
+        for kv, ref in enumerate((k_hbm, v_hbm)):
+
+            @pl.when(core == 0)
+            def _():
+                copy(SIB_OWN, ref, N1, head, kv, sibling).start()
+
+        return carry
+
     def send_own(head, carry):
         for kv, ref in enumerate((k_hbm, v_hbm)):
 
@@ -160,10 +211,6 @@
             def _():
                 copy(OWN_B, ref, N4, head, kv, at(seg, x + 2, core)).start()
 
-            @pl.when(core == 0)
-            def _():
-                copy(SIB_OWN, ref, N1, head, kv, sibling).start()
-
         return carry
 
     def send_over(head, carry):
@@ -186,7 +233,7 @@
         return carry
 
     lax.fori_loop(0, head_count, send_over, 0)
-    lax.fori_loop(0, head_count, send_own, 0)
+    lax.fori_loop(0, head_count, send_sibling, 0)
     lax.fori_loop(0, head_count, pass_on, 0)
     for number in range(4):
 
@@ -194,56 +241,8 @@
         def _():
             slot[number] = jnp.zeros(slot.shape[1:], slot.dtype)
 
-    for one in loads:
+    for one in loads[:3]:
         one.wait()
-
-    def transpose_pair(pair, carry):
-        columns = pl.ds(pl.multiple_of(pair * 2 * cols, 128), 2 * cols)
-        found = jnp.transpose(w_ref[:, columns])
-        wt[2 * pair] = found[:cols]
-        wt[2 * pair + 1] = found[cols:]
-        return carry
-
-    lax.fori_loop(0, n // 2, transpose_pair, 0)
-
-    def region(y_of, x_of, core_of):
-        return y_of * 8 + core_of * 4 + x_of
-
-    def region_rows(number):
-        return pl.ds(pl.multiple_of(number * w_rows, 16), w_rows)
-
-    def there(number):
-        return number * w_rows < cols
-
-    mine = region(y, x, core)
-
-    def z_copy(other):
-        return remote(
-            wt.at[other, region_rows(mine)],
-            wc.at[me, region_rows(mine)],
-            z_send.at[other],
-            z_recv.at[me],
-            (ctx, other),
-        )
-
-    def z_arrival(other):
-        return remote(
-            wt.at[other, region_rows(mine)],
-            wc.at[other, region_rows(mine)],
-            z_send.at[other],
-            z_recv.at[other],
-            (ctx, other),
-        )
-
-    @pl.when(there(mine))
-    def _():
-        wc[me, region_rows(mine)] = wt[me, region_rows(mine)]
-
-        def start(step, carry):
-            z_copy(lax.rem(me + step, n)).start()
-            return carry
-
-        lax.fori_loop(1, n, start, 0)
 
     def w_copy(number, send_sem, device):
         rows_of = region_rows(number)
@@ -397,13 +396,6 @@
         return jnp.dot(keys, qx[head], preferred_element_type=jnp.float32)
 
     def own_block(head, carry):
-        for kv in range(2):
-
-            @pl.when(x == 1)
-            def _():
-                arrived(N2, head, kv)
-                copy(SECOND, slot.at[N2, kv], N4, head, kv, at(seg, 2, core)).start()
-
         found = score(part_of(own.at[0], head)[...], -1, head)
         allowed = (key_at <= query_at) & (key_at >= start)
         found = jnp.where(allowed, found, NEVER)
@@ -416,9 +408,21 @@
         )
         return carry
 
-    lax.fori_loop(0, head_count, own_block, 0)
+    lax.fori_loop(0, head_count // 2, own_block, 0)
     x_stage()
+    lax.fori_loop(0, head_count, send_own, 0)
+    lax.fori_loop(head_count // 2, head_count, own_block, 0)
     y_stage()
+
+    def hand_on(head, carry):
+        for kv in range(2):
+            arrived(N2, head, kv)
+            copy(SECOND, slot.at[N2, kv], N4, head, kv, at(seg, 2, core)).start()
+        return carry
+
+    @pl.when(x == 1)
+    def _():
+        lax.fori_loop(0, head_count, hand_on, 0)
 
     def bring(head, kv):
         @pl.when((ctx >= 2) & (x != 1))
@@ -465,16 +469,6 @@
             probs[number] = weights.astype(jnp.bfloat16)
         bring(head, 1)
 
-        @pl.when((head == head_count - 1) & gives)
-        def _():
-            for x_of in (2, 3):
-                pl.semaphore_signal(go, inc=1, device_id=at(seg, x_of, core), device_id_type=MESH)
-
-        @pl.when((head == head_count - 1) & gives_first)
-        def _():
-            for x_of in range(4):
-                pl.semaphore_signal(go, inc=1, device_id=at(0, x_of, core), device_id_type=MESH)
-
         summed = part_of(acc, head)[...] * factor
         for number in range(4):
             summed = summed + jnp.dot(
@@ -489,10 +483,6 @@
 
     lax.fori_loop(0, head_count, earlier_blocks, 0)
 
-    @pl.when(held)
-    def _():
-        pl.semaphore_wait(go, 1)
-
     places = ((ctx, me + 1), (ctx, me - 1))
     below = (me, n - 1 - me)
 
@@ -519,14 +509,14 @@
     c_stage()
 
     def partials(owner, carry):
-        found = jnp.dot(wt[owner], first_half[...], preferred_element_type=jnp.float32).astype(jnp.bfloat16)
+        found = jnp.dot(wt[owner, :, :cols], first_half[...], preferred_element_type=jnp.float32).astype(jnp.bfloat16)
         for piece in range(2):
             part[owner, piece] = found[:, piece * piece_len : (piece + 1) * piece_len]
         return carry
 
     lax.fori_loop(0, n, partials, 0)
     for piece in range(2):
-        second_half[piece] = jnp.dot(wt[me], spread[me, piece], preferred_element_type=jnp.float32)
+        second_half[piece] = jnp.dot(wt[me, :, :cols], spread[me, piece], preferred_element_type=jnp.float32)
     def slot_of(time, carry):
         number, piece = lax.div(time, 2), lax.rem(time, 2)
         for way in (UP, DOWN):
@@ -566,7 +556,9 @@
 
             @pl.when(number <= below[way])
             def _():
-                second_half[piece] += jnp.dot(wc[source], spread[source, piece], preferred_element_type=jnp.float32)
+                second_half[piece] += jnp.dot(
+                    wc[source, :, :cols], spread[source, piece], preferred_element_type=jnp.float32
+                )
 
         return carry
 
@@ -637,6 +629,7 @@
     y_count = max(1, lax.axis_size("ctx") // 16)
     regions = 8 * y_count
     piece = rows // PIECES
+    lanes = 128 * -(-cols // 128)
     bf16, f32 = jnp.bfloat16, jnp.float32
     vmem, smem = pl.BlockSpec(memory_space=pltpu.VMEM), pl.BlockSpec(memory_space=pltpu.SMEM)
     anywhere = pl.BlockSpec(memory_space=pl.ANY)
@@ -657,8 +650,8 @@
             pltpu.VMEM((cols, rows), f32),
             pltpu.VMEM((heads, 1, rows), f32),
             pltpu.VMEM((heads, 1, rows), f32),
-            pltpu.VMEM((n, cols, cols), bf16),
-            pltpu.VMEM((n, cols, cols), bf16),
+            pltpu.VMEM((n, cols, lanes), bf16),
+            pltpu.VMEM((n, cols, lanes), bf16),
             pltpu.VMEM((cols, 2 * piece), bf16),
             pltpu.VMEM((n, 2, cols, piece), bf16),
             pltpu.VMEM((n, 2, cols, piece), bf16),
@@ -677,7 +670,6 @@
             dma((n, 2)),
             dma((n, 2)),
             dma((2, n, 2)),
-            pltpu.SemaphoreType.REGULAR,
         ],
         compiler_params=pltpu.CompilerParams(
             collective_id=0, has_side_effects=True, vmem_limit_bytes=56 << 20

time: 149 us -> 141 us (0.946)
  the two profiles are of different devices: /device:TPU:4 before, /device:TPU:19 now
where the time goes in v4:
time: 141 us
  Pallas kernels  139 us (99%)
  local copies, waits for them, and re-layouts  1.82 us (1%)
    pallas_call x1, Pallas kernels, layer(): pl.pallas_call(layer_kernel, out_shape=jax.ShapeDtypeStruct((cols, rows),...  139 us

profile of v4, /device:TPU:19, one launch (start us, length us, event | category | flops | bytes accessed | tf_op | source)
XLA Modules:
  0.0 140.7 jit_solution(1316938896542825465)
XLA Ops:
  0.0 138.9 %shard_map.64 = bf16[448,512]{1,0:T(8,128)(2,1)} custom-call(s32[32]{0:T(128)} %docs_ref.1, f32[128]{0:T(128)} %constant.2.clone.slopes_ref, bf16[448,512]{1,0:T(8,128)(2,1)} %bitcast.5, bf16[448,512]{1,0:T(8,128)(2,1)} %bitcast.6, bf16[448,512]{1,0:T(8,128)(2,1)} %bitcast.7, bf16[448,3584]{1,0:T(8,128)(2,1)} %w_hbm.1), custom_call_target="tpu_custom_call" | custom-call | tf_op jit(solution)/shard_map/pallas_call | solution.py:637
  138.9 1.8 %copy.8 = bf16[512,448]{0,1:T(8,128)(2,1)} copy(bf16[512,448]{0,1:T(8,128)(2,1)} %bitcast.4) | data formatting | bytes 917504

commit v5 on v4

--- a/solution.py
+++ b/solution.py
@@ -408,11 +408,10 @@
         )
         return carry
 
+    lax.fori_loop(0, head_count, send_own, 0)
+    x_stage()
     lax.fori_loop(0, head_count // 2, own_block, 0)
-    x_stage()
-    lax.fori_loop(0, head_count, send_own, 0)
     lax.fori_loop(head_count // 2, head_count, own_block, 0)
-    y_stage()
 
     def hand_on(head, carry):
         for kv in range(2):
@@ -424,19 +423,20 @@
     def _():
         lax.fori_loop(0, head_count, hand_on, 0)
 
+    def hand_out(head, kv):
+        @pl.when((ctx >= 2) & (x != 1))
+        def _():
+            arrived(N2, head, kv)
+
+        @pl.when((x == 0) & has_prev)
+        def _():
+            copy(SECOND, slot.at[N2, kv], N4, head, kv, at(seg, 1, core)).start()
+
+        @pl.when(ctx >= 2)
+        def _():
+            copy(SIB_N2, slot.at[N2, kv], jnp.where(core == 0, N3, N1), head, kv, sibling).start()
+
     def bring(head, kv):
-        @pl.when((ctx >= 2) & (x != 1))
-        def _():
-            arrived(N2, head, kv)
-
-        @pl.when(ctx >= 2)
-        def _():
-            copy(SIB_N2, slot.at[N2, kv], jnp.where(core == 0, N3, N1), head, kv, sibling).start()
-
-        @pl.when((x == 0) & has_prev)
-        def _():
-            copy(SECOND, slot.at[N2, kv], N4, head, kv, at(seg, 1, core)).start()
-
         @pl.when(ctx >= 4)
         def _():
             arrived(N4, head, kv)
@@ -454,6 +454,8 @@
             arrived(N3, head, kv)
 
     def earlier_blocks(head, carry):
+        hand_out(head, 0)
+        hand_out(head, 1)
         bring(head, 0)
         most = top[head]
         for number in range(4):
@@ -506,7 +508,7 @@
             def _():
                 spread_copy(way, me, piece).start()
 
-    c_stage()
+    y_stage()
 
     def partials(owner, carry):
         found = jnp.dot(wt[owner, :, :cols], first_half[...], preferred_element_type=jnp.float32).astype(jnp.bfloat16)
@@ -562,11 +564,12 @@
 
         return carry
 
-    lax.fori_loop(2, 2 + lag, slot_of, 0)
+    late = max(2, 2 * n - 4)
+    lax.fori_loop(2, late, slot_of, 0)
+    c_stage()
+    lax.fori_loop(late, 2 * n, slot_of, 0)
     c_arrivals()
-    lax.fori_loop(2 + lag, 2 * n, lambda time, carry: product(time - lag, slot_of(time, carry)), 0)
-    lax.fori_loop(2 * n - lag, 2 * n, product, 0)
-
+    lax.fori_loop(2, 2 * n, product, 0)
     for piece in range(2):
         for way in (UP, DOWN):
 

time: 141 us -> 136 us (0.965)
  the two profiles are of different devices: /device:TPU:19 before, /device:TPU:386 now
where the time goes in v5:
time: 136 us
  Pallas kernels  134 us (99%)
  local copies, waits for them, and re-layouts  1.82 us (1%)
    pallas_call x1, Pallas kernels, layer(): pl.pallas_call(layer_kernel, out_shape=jax.ShapeDtypeStruct((cols, rows),...  134 us

profile of v5, /device:TPU:386, one launch (start us, length us, event | category | flops | bytes accessed | tf_op | source)
XLA Modules:
  0.0 135.8 jit_solution(13917443408177072790)
XLA Ops:
  0.0 134.0 %shard_map.64 = bf16[448,512]{1,0:T(8,128)(2,1)} custom-call(s32[32]{0:T(128)} %docs_ref.1, f32[128]{0:T(128)} %constant.2.clone.slopes_ref, bf16[448,512]{1,0:T(8,128)(2,1)} %bitcast.5, bf16[448,512]{1,0:T(8,128)(2,1)} %bitcast.6, bf16[448,512]{1,0:T(8,128)(2,1)} %bitcast.7, bf16[448,3584]{1,0:T(8,128)(2,1)} %w_hbm.1), custom_call_target="tpu_custom_call" | custom-call | tf_op jit(solution)/shard_map/pallas_call | solution.py:640
  134.0 1.8 %copy.8 = bf16[512,448]{0,1:T(8,128)(2,1)} copy(bf16[512,448]{0,1:T(8,128)(2,1)} %bitcast.4) | data formatting | bytes 917504

commit v6 on v5

--- a/solution.py
+++ b/solution.py
@@ -119,7 +119,6 @@
     for one in loads:
         one.start()
 
-    loads[3].wait()
     def transpose_pair(pair, carry):
         columns = pl.ds(pl.multiple_of(pair * 2 * cols, 128), 2 * cols)
         found = jnp.transpose(w_ref[:, columns])
@@ -127,7 +126,6 @@
         wt[2 * pair + 1, :, :cols] = found[cols:]
         return carry
 
-    lax.fori_loop(0, n // 2, transpose_pair, 0)
     crossing = crosses.astype(jnp.int32) + passes.astype(jnp.int32)
     awaited = 1 + 3 + (y_count - 1) + (n - 1) + crossing
     pl.semaphore_wait(barrier, awaited)
@@ -165,16 +163,6 @@
             z_recv.at[other],
             (ctx, other),
         )
-
-    @pl.when(there(mine))
-    def _():
-        wc[me, region_rows(mine)] = wt[me, region_rows(mine)]
-
-        def start(step, carry):
-            z_copy(lax.rem(me + step, n)).start()
-            return carry
-
-        lax.fori_loop(1, n, start, 0)
 
     def part_of(ref, head):
         return ref.at[pl.ds(pl.multiple_of(head * HD, 16), HD)]
@@ -409,7 +397,19 @@
         return carry
 
     lax.fori_loop(0, head_count, send_own, 0)
-    x_stage()
+    loads[3].wait()
+    lax.fori_loop(0, n // 2, transpose_pair, 0)
+
+    @pl.when(there(mine))
+    def _():
+        wc[me, region_rows(mine)] = wt[me, region_rows(mine)]
+
+        def start(step, carry):
+            z_copy(lax.rem(me + step, n)).start()
+            return carry
+
+        lax.fori_loop(1, n, start, 0)
+
     lax.fori_loop(0, head_count // 2, own_block, 0)
     lax.fori_loop(head_count // 2, head_count, own_block, 0)
 
@@ -508,7 +508,7 @@
             def _():
                 spread_copy(way, me, piece).start()
 
-    y_stage()
+    x_stage()
 
     def partials(owner, carry):
         found = jnp.dot(wt[owner, :, :cols], first_half[...], preferred_element_type=jnp.float32).astype(jnp.bfloat16)
@@ -564,8 +564,11 @@
 
         return carry
 
-    late = max(2, 2 * n - 4)
-    lax.fori_loop(2, late, slot_of, 0)
+    soon = min(6, 2 * n)
+    late = max(soon, 2 * n - 2)
+    lax.fori_loop(2, soon, slot_of, 0)
+    y_stage()
+    lax.fori_loop(soon, late, slot_of, 0)
     c_stage()
     lax.fori_loop(late, 2 * n, slot_of, 0)
     c_arrivals()

time: 136 us -> 136 us (level)
  no operation moved by 1% of the time
where the time goes in v6:
time: 136 us
  Pallas kernels  134 us (99%)
  local copies, waits for them, and re-layouts  1.82 us (1%)
    pallas_call x1, Pallas kernels, layer(): pl.pallas_call(layer_kernel, out_shape=jax.ShapeDtypeStruct((cols, rows),...  134 us

profile of v6, /device:TPU:386, one launch (start us, length us, event | category | flops | bytes accessed | tf_op | source)
XLA Modules:
  0.0 136.2 jit_solution(16961096249603811107)
XLA Ops:
  0.0 134.4 %shard_map.64 = bf16[448,512]{1,0:T(8,128)(2,1)} custom-call(s32[32]{0:T(128)} %docs_ref.1, f32[128]{0:T(128)} %constant.2.clone.slopes_ref, bf16[448,512]{1,0:T(8,128)(2,1)} %bitcast.5, bf16[448,512]{1,0:T(8,128)(2,1)} %bitcast.6, bf16[448,512]{1,0:T(8,128)(2,1)} %bitcast.7, bf16[448,3584]{1,0:T(8,128)(2,1)} %w_hbm.1), custom_call_target="tpu_custom_call" | custom-call | tf_op jit(solution)/shard_map/pallas_call | solution.py:643
  134.4 1.8 %copy.8 = bf16[512,448]{0,1:T(8,128)(2,1)} copy(bf16[512,448]{0,1:T(8,128)(2,1)} %bitcast.4) | data formatting | bytes 917504
